TPU v7x, 256 devices: a whole 4x4x8 slice. The times are simulated.
256 devices in a mesh: blk: 8 (over x, y_lo), grp: 32 (over z, y_hi, core).
Axes of the slice: x: 4, y: 4 (y_hi: 2, y_lo: 2; y = y_hi * 2 + y_lo), z: 8, core: 2. Of those that a mesh axis runs over, the one named last changes fastest.
Arguments:
- features: bfloat16 [65536, 256], P(('blk', 'grp')), may hold values from -6 to 6
- blocks: bfloat16 [8, 32, 8, 24, 128, 128], P('blk', 'grp'), may hold values from -1.5 to 1.5
- block_pos: int32 [8, 32, 8, 24], P('blk', 'grp'), may hold values from 0 to 127
- counts: int32 [8, 32, 8], P('blk', 'grp'), may hold values from 1 to 24, as said below
- degree: int32 [65536], P(('blk', 'grp')), may hold values from 8 to 64
- w_self: bfloat16 [256, 256], replicated, may hold values from -0.375 to 0.375
- w_neigh: bfloat16 [256, 256], replicated, may hold values from -0.375 to 0.375
- cotangent: bfloat16 [65536, 256], P(('blk', 'grp')), may hold values from -6 to 6
Outputs:
- out: bfloat16 [65536, 256], P(('blk', 'grp'))
- grad_x: bfloat16 [65536, 256], P(('blk', 'grp'))
- grad_self: float32 [256, 256], replicated
- grad_neigh: float32 [256, 256], replicated
Inputs may be any that keep to these rules, and one draw needn't show every extreme that they name: `counts`: every list holds at least one live block; on every device some list is full with 24 live blocks, and lists differ by up to a factor of eight in their live blocks. `block_pos`: positions may repeat inside a list; blocks of repeated positions add.
All inputs are finite; a program needn't handle non-finite values.
Results may differ from a plain program's by a relative error of at most 0.025.
Values may be sent and summed in bfloat16 or wider, within the bound.
No kernel may reach another device: no remote copies, remote signals or barrier semaphores. Data moves between devices by JAX's collectives and lax.ppermute only.
A program may use at most 128 MiB of HBM per device.

v0:
```python
import math

import jax
import jax.numpy as jnp
from jax import lax
from jax.sharding import PartitionSpec as P


def passed_along(block, axis, distance):
    devices = range(lax.axis_size(axis))
    route = [((i - distance) % len(devices), i) for i in devices]
    return lax.ppermute(block, axis, route)


def slab_kernel(running, block_values, block_places, live_count, first_slot, feat_piece):
    tile_size = block_values.shape[-1]
    col_count = feat_piece.shape[0] // tile_size
    col_tiles = feat_piece.reshape(col_count, tile_size, feat_piece.shape[1])
    picked = col_tiles[block_places % col_count]
    products = jnp.einsum("jab,jbf->jaf", block_values, picked, preferred_element_type=jnp.float32)
    slot_ids = first_slot + jnp.arange(block_places.shape[0], dtype=jnp.int32)
    products = jnp.where((slot_ids < live_count)[:, None, None], products, 0.0)
    return running.at[block_places // col_count].add(products)


def class_kernel(running, block_values, block_places, live_count, first_slot, grad_tiles):
    col_count = running.shape[0]
    picked = grad_tiles[block_places // col_count]
    products = jnp.einsum("jab,jaf->jbf", block_values, picked, preferred_element_type=jnp.float32)
    slot_ids = first_slot + jnp.arange(block_places.shape[0], dtype=jnp.int32)
    products = jnp.where((slot_ids < live_count)[:, None, None], products, 0.0)
    return running.at[block_places % col_count].add(products)


def over_slots(kernel, initial, block_values, block_places, live_count, operand):
    return kernel(initial, block_values, block_places, live_count, 0, operand)


def per_device(features, blocks, block_pos, counts, degree, w_self, w_neigh, cotangent):
    cycle_size = lax.axis_size("blk")
    group_size = lax.axis_size("grp")
    row_count, feat_width = features.shape
    tile_size = blocks.shape[-1]
    col_count = row_count // tile_size
    tile_rows = group_size * col_count
    block_values = blocks[0, 0]
    block_places = block_pos[0, 0]
    live_counts = counts[0, 0]
    running = jnp.zeros((tile_rows, tile_size, feat_width), jnp.float32)
    current = features
    for offset in range(cycle_size):
        running = over_slots(
            slab_kernel,
            running,
            block_values[offset],
            block_places[offset],
            live_counts[offset],
            current,
        )
        if offset + 1 < cycle_size:
            current = passed_along(current, "blk", 1)
    partial_rows = running.reshape(tile_rows * tile_size, feat_width).astype(jnp.bfloat16)
    summed = lax.psum_scatter(partial_rows, "grp", scatter_dimension=0, tiled=True).astype(
        jnp.float32
    )
    scale_deg = degree.astype(jnp.float32)[:, None]
    mean_feats = (summed / scale_deg).astype(jnp.bfloat16)
    pre_act = jnp.dot(features, w_self, preferred_element_type=jnp.float32) + jnp.dot(
        mean_feats, w_neigh, preferred_element_type=jnp.float32
    )
    out = jax.nn.silu(pre_act).astype(jnp.bfloat16)
    sigma = jax.nn.sigmoid(pre_act)
    grad_pre = (cotangent.astype(jnp.float32) * sigma * (1.0 + pre_act * (1.0 - sigma))).astype(
        jnp.bfloat16
    )
    transposed = (((1,), (1,)), ((), ()))
    grad_slab = (
        lax.dot_general(grad_pre, w_neigh, transposed, preferred_element_type=jnp.float32)
        / scale_deg
    ).astype(jnp.bfloat16)
    whole_grads = lax.all_gather(grad_slab, "grp", axis=0, tiled=True).reshape(
        tile_rows, tile_size, feat_width
    )

    def class_term(offset):
        empty = jnp.zeros((col_count, tile_size, feat_width), jnp.float32)
        part_sum = over_slots(
            class_kernel,
            empty,
            block_values[offset],
            block_places[offset],
            live_counts[offset],
            whole_grads,
        )
        return part_sum.reshape(row_count, feat_width)

    back_sum = class_term(cycle_size - 1)
    for offset in range(cycle_size - 2, -1, -1):
        back_sum = passed_along(back_sum.astype(jnp.bfloat16), "blk", -1).astype(
            back_sum.dtype
        ) + class_term(offset)
    grad_x = (
        lax.dot_general(grad_pre, w_self, transposed, preferred_element_type=jnp.float32) + back_sum
    ).astype(jnp.bfloat16)
    over_rows = (((0,), (0,)), ((), ()))
    local_self = lax.dot_general(features, grad_pre, over_rows, preferred_element_type=jnp.float32)
    local_neigh = lax.dot_general(
        mean_feats, grad_pre, over_rows, preferred_element_type=jnp.float32
    )
    total_self, total_neigh = lax.psum((local_self, local_neigh), ("blk", "grp"))
    norm_scale = 1.0 / math.sqrt(row_count * cycle_size * group_size)
    return (out, grad_x, total_self * norm_scale, total_neigh * norm_scale)


def solution(mesh):
    in_specs = (
        P(("blk", "grp"), None),
        P("blk", "grp", None, None, None, None),
        P("blk", "grp", None, None),
        P("blk", "grp", None),
        P(("blk", "grp")),
        P(),
        P(),
        P(("blk", "grp"), None),
    )
    out_specs = (P(("blk", "grp"), None), P(("blk", "grp"), None), P(), P())
    return jax.shard_map(
        per_device, mesh=mesh, in_specs=in_specs, out_specs=out_specs, check_vma=False
    )
```

profile of v0, /device:TPU:2, one launch (start us, length us, event | category | flops | bytes accessed | tf_op | source)
XLA Modules:
  0.0 779.8 jit_solution(15350095654619150363)
XLA Ops:
  20.1 2.8 gather_fusion
  27.0 2.4 copy.32
  29.4 4.3 broadcast_in_dim.138
  33.7 8.6 %scatter_fusion = f32[64,128,256]{2,1,0:T(8,128)} fusion(f32[64,128,256]{2,1,0:T(8,128)} %broadcast_in_dim.138, s32[24]{0:T(128)S(1)} %get-tuple-element.33, f32[24,128,256]{2,1,0:T(8,128)S(1)} %copy-done.3), kind=kCustom, calls=%fused_computation.16 | custom fusion | flops 786432 | bytes 9437280 | tf_op jit(solution)/shard_map/scatter-add | solution.py:23
  44.6 3.6 select_bitcast_fusion.14
  50.6 8.9 %scatter_fusion.1 = f32[64,128,256]{2,1,0:T(8,128)} fusion(f32[64,128,256]{2,1,0:T(8,128)} %scatter_fusion, s32[24]{0:T(128)} %get-tuple-element.34, f32[24,128,256]{2,1,0:T(8,128)S(1)} %copy.34), kind=kCustom, calls=%fused_computation.17 | custom fusion | flops 786432 | bytes 9437280 | tf_op jit(solution)/shard_map/scatter-add | solution.py:23
  61.7 3.6 select_bitcast_fusion.13
  67.6 8.8 %scatter_fusion.2 = f32[64,128,256]{2,1,0:T(8,128)} fusion(f32[64,128,256]{2,1,0:T(8,128)} %scatter_fusion.1, s32[24]{0:T(128)} %get-tuple-element.35, f32[24,128,256]{2,1,0:T(8,128)S(1)} %copy.36), kind=kCustom, calls=%fused_computation.18 | custom fusion | flops 786432 | bytes 9437280 | tf_op jit(solution)/shard_map/scatter-add | solution.py:23
  78.6 3.6 select_bitcast_fusion.12
  84.5 8.7 %scatter_fusion.3 = f32[64,128,256]{2,1,0:T(8,128)} fusion(f32[64,128,256]{2,1,0:T(8,128)} %scatter_fusion.2, s32[24]{0:T(128)} %get-tuple-element.36, f32[24,128,256]{2,1,0:T(8,128)S(1)} %copy.38), kind=kCustom, calls=%fused_computation.19 | custom fusion | flops 786432 | bytes 9437280 | tf_op jit(solution)/shard_map/scatter-add | solution.py:23
  95.9 3.6 select_bitcast_fusion.11
  99.5 2.4 copy.40
  101.9 8.7 %scatter_fusion.4 = f32[64,128,256]{2,1,0:T(8,128)} fusion(f32[64,128,256]{2,1,0:T(8,128)} %scatter_fusion.3, s32[24]{0:T(128)S(1)} %copy-done.24, f32[24,128,256]{2,1,0:T(8,128)S(1)} %copy.40), kind=kCustom, calls=%fused_computation.20 | custom fusion | flops 786432 | bytes 9437280 | tf_op jit(solution)/shard_map/scatter-add | solution.py:23
  113.3 3.6 select_bitcast_fusion.10
  119.3 8.7 %scatter_fusion.5 = f32[64,128,256]{2,1,0:T(8,128)} fusion(f32[64,128,256]{2,1,0:T(8,128)} %scatter_fusion.4, s32[24]{0:T(128)S(1)} %copy-done.25, f32[24,128,256]{2,1,0:T(8,128)S(1)} %copy.42), kind=kCustom, calls=%fused_computation.21 | custom fusion | flops 786432 | bytes 9437280 | tf_op jit(solution)/shard_map/scatter-add | solution.py:23
  129.2 3.6 select_bitcast_fusion.9
  135.2 8.7 %scatter_fusion.6 = f32[64,128,256]{2,1,0:T(8,128)} fusion(f32[64,128,256]{2,1,0:T(8,128)} %scatter_fusion.5, s32[24]{0:T(128)S(1)} %copy-done.27, f32[24,128,256]{2,1,0:T(8,128)S(1)} %copy.44), kind=kCustom, calls=%fused_computation.22 | custom fusion | flops 786432 | bytes 9437280 | tf_op jit(solution)/shard_map/scatter-add | solution.py:23
  144.6 3.6 select_bitcast_fusion.8
  150.5 8.9 %scatter_fusion.7 = f32[64,128,256]{2,1,0:T(8,128)} fusion(f32[64,128,256]{2,1,0:T(8,128)} %scatter_fusion.6, s32[24]{0:T(128)S(1)} %copy-done.26, f32[24,128,256]{2,1,0:T(8,128)S(1)} %copy.46), kind=kCustom, calls=%fused_computation.23 | custom fusion | flops 786432 | bytes 9437280 | tf_op jit(solution)/shard_map/scatter-add | solution.py:23
  159.5 6.0 convert_element_type.75
  166.7 129.5 %reduce-scatter.2.cloned.1.call-done = bf16[256,256]{1,0:T(8,128)(2,1)} async-done(((bf16[8192,256]{1,0:T(8,128)(2,1)}), bf16[256,256]{1,0:T(8,128)(2,1)}) %reduce-scatter.2.cloned.1.call-update) | async-done | bytes 131088 | tf_op jit(solution)/shard_map/reduce_scatter | solution.py:63
  303.2 250.5 %all-reduce.3.cloned.1.call-done = (f32[256,256]{0,1:T(8,128)}, f32[256,256]{0,1:T(8,128)}) async-done(((f32[256,256]{0,1:T(8,128)}, f32[256,256]{0,1:T(8,128)}), (f32[256,256]{0,1:T(8,128)}, f32[256,256]{0,1:T(8,128)})) %all-reduce.3.cloned.1.call-update) | async-done | bytes 524304 | tf_op jit(solution)/shard_map/psum | solution.py:110
  556.5 86.5 %all-gather.2.cloned.1.call-done = bf16[8192,256]{1,0:T(8,128)(2,1)} async-done(((bf16[256,256]{1,0:T(8,128)(2,1)}), bf16[8192,256]{1,0:T(8,128)(2,1)}) %all-gather.2.cloned.1.call-update) | async-done | bytes 4194320 | tf_op jit(solution)/shard_map/all_gather | solution.py:81
  643.0 2.8 gather_fusion.8
  645.9 3.6 select_bitcast_fusion.7
  651.8 3.7 scatter_fusion.8
  656.4 3.0 gather_fusion.9
  659.4 3.6 select_bitcast_fusion.6
  665.3 4.2 gather_fusion.10
  669.6 3.9 scatter_fusion.9
  675.9 4.1 select_bitcast_fusion.5
  682.4 4.2 gather_fusion.11
  686.6 3.9 scatter_fusion.10
  691.4 2.8 collective-permute-start.9
  694.2 4.1 select_bitcast_fusion.4
  700.7 4.1 gather_fusion.12
  704.8 3.9 scatter_fusion.11
  711.4 4.0 select_bitcast_fusion.3
  717.8 4.1 gather_fusion.13
  721.9 3.7 scatter_fusion.12
  727.6 4.0 select_bitcast_fusion.2
  734.0 4.1 gather_fusion.14
  738.1 3.7 scatter_fusion.13
  744.3 4.0 select_bitcast_fusion.1
  750.7 4.1 gather_fusion.15
  754.9 3.7 scatter_fusion.14
  761.0 4.0 select_bitcast_fusion
  767.4 3.7 scatter_fusion.15
  (192 shorter events, 90.4 us)
Async XLA Ops:
  7.2 289.0 %copy-start = (bf16[256,256]{1,0:T(8,128)(2,1)S(1)}, bf16[256,256]{1,0:T(8,128)(2,1)}, u32[]{:S(2)}) copy-start(bf16[256,256]{1,0:T(8,128)(2,1)} %param.14) | copy-start | bytes 393220
  7.2 289.0 %reduce-scatter.2.cloned.1.call-start = ((), (), s32[]{:S(2)}) async-start(), calls=%async_computation.1 | async-start | bytes 4325376 | tf_op jit(solution)/shard_map/reduce_scatter | solution.py:63
  7.2 35.1 %collective-permute-start = (bf16[256,256]{1,0:T(8,128)(2,1)}, bf16[256,256]{1,0:T(8,128)(2,1)S(1)}, u32[]{:S(2)}, u32[]{:S(2)}) collective-permute-start(bf16[256,256]{1,0:T(8,128)(2,1)} %param.8), channel_id=1, source_target_pairs={{224,0},{0,32},{32,64},{64,96},{96,128},{128,160},{160,192},{192,2... | collective-permute-start | bytes 393224 | tf_op jit(solution)/shard_map/ppermute | solution.py:12
  9.9 10.2 %copy-start.6 = (s32[24]{0:T(128)}, s32[24]{0:T(128)S(1)}, u32[]{:S(2)}) copy-start(s32[24]{0:T(128)S(1)} %get-tuple-element.50) | copy-start | bytes 292
  9.9 15.4 %copy-start.8 = (s32[24]{0:T(128)}, s32[24]{0:T(128)S(1)}, u32[]{:S(2)}) copy-start(s32[24]{0:T(128)S(1)} %get-tuple-element.48) | copy-start | bytes 292
  9.9 15.4 %copy-start.10 = (s32[24]{0:T(128)}, s32[24]{0:T(128)S(1)}, u32[]{:S(2)}) copy-start(s32[24]{0:T(128)S(1)} %get-tuple-element.46) | copy-start | bytes 292
  9.9 15.4 %copy-start.12 = (s32[24]{0:T(128)}, s32[24]{0:T(128)S(1)}, u32[]{:S(2)}) copy-start(s32[24]{0:T(128)S(1)} %get-tuple-element.44) | copy-start | bytes 292
  9.9 15.4 %copy-start.14 = (s32[24]{0:T(128)}, s32[24]{0:T(128)S(1)}, u32[]{:S(2)}) copy-start(s32[24]{0:T(128)S(1)} %get-tuple-element.42) | copy-start | bytes 292
  9.9 15.4 %copy-start.15 = (s32[24]{0:T(128)}, s32[24]{0:T(128)S(1)}, u32[]{:S(2)}) copy-start(s32[24]{0:T(128)S(1)} %get-tuple-element.40) | copy-start | bytes 292
  9.9 15.4 %copy-start.16 = (s32[24]{0:T(128)}, s32[24]{0:T(128)S(1)}, u32[]{:S(2)}) copy-start(s32[24]{0:T(128)S(1)} %get-tuple-element.52) | copy-start | bytes 292
  10.0 32.4 %copy-start.17 = (s32[24]{0:T(128)}, s32[24]{0:T(128)S(1)}, u32[]{:S(2)}) copy-start(s32[24]{0:T(128)S(1)} %get-tuple-element.14) | copy-start | bytes 292
  12.2 13.1 %copy-start.28 = (pred[24]{0:T(512)(128)(4,1)}, pred[24]{0:T(512)(128)(4,1)S(1)}, u32[]{:S(2)}) copy-start(pred[24]{0:T(512)(128)(4,1)S(1)} %iota_compare_fusion.7) | copy-start | bytes 76
  12.9 31.7 %copy-start.30 = (pred[24]{0:T(512)(128)(4,1)}, pred[24]{0:T(512)(128)(4,1)S(1)}, u32[]{:S(2)}) copy-start(pred[24]{0:T(512)(128)(4,1)S(1)} %iota_compare_fusion.6) | copy-start | bytes 76
  22.9 2.4 copy-start.5
  25.9 7.8 copy-start.19
  29.4 4.3 copy-start.3
  43.0 16.5 %collective-permute-start.1 = (bf16[256,256]{1,0:T(8,128)(2,1)S(1)}, bf16[256,256]{1,0:T(8,128)(2,1)S(1)}, u32[]{:S(2)}, u32[]{:S(2)}) collective-permute-start(bf16[256,256]{1,0:T(8,128)(2,1)S(1)} %collective-permute-done), channel_id=1, source_target_pairs={{224,0},{0,32},{32,64},{64,96},{96,128},{128,160},{160,192},{192,2... | collective-permute-start | bytes 393224 | tf_op jit(solution)/shard_map/ppermute | solution.py:12
  60.3 16.2 %collective-permute-start.2 = (bf16[256,256]{1,0:T(8,128)(2,1)S(1)}, bf16[256,256]{1,0:T(8,128)(2,1)S(1)}, u32[]{:S(2)}, u32[]{:S(2)}) collective-permute-start(bf16[256,256]{1,0:T(8,128)(2,1)S(1)} %collective-permute-done.1), channel_id=1, source_target_pairs={{224,0},{0,32},{32,64},{64,96},{96,128},{128,160},{160,192},{192,2... | collective-permute-start | bytes 393224 | tf_op jit(solution)/shard_map/ppermute | solution.py:12
  77.2 16.1 %collective-permute-start.3 = (bf16[256,256]{1,0:T(8,128)(2,1)S(1)}, bf16[256,256]{1,0:T(8,128)(2,1)S(1)}, u32[]{:S(2)}, u32[]{:S(2)}) collective-permute-start(bf16[256,256]{1,0:T(8,128)(2,1)S(1)} %collective-permute-done.2), channel_id=1, source_target_pairs={{224,0},{0,32},{32,64},{64,96},{96,128},{128,160},{160,192},{192,2... | collective-permute-start | bytes 393224 | tf_op jit(solution)/shard_map/ppermute | solution.py:12
  93.3 2.7 copy-start.36
  93.9 16.7 %collective-permute-start.4 = (bf16[256,256]{1,0:T(8,128)(2,1)S(1)}, bf16[256,256]{1,0:T(8,128)(2,1)S(1)}, u32[]{:S(2)}, u32[]{:S(2)}) collective-permute-start(bf16[256,256]{1,0:T(8,128)(2,1)S(1)} %collective-permute-done.3), channel_id=1, source_target_pairs={{224,0},{0,32},{32,64},{64,96},{96,128},{128,160},{160,192},{192,2... | collective-permute-start | bytes 393224 | tf_op jit(solution)/shard_map/ppermute | solution.py:12
  110.6 2.7 copy-start.37
  111.3 16.7 %collective-permute-start.5 = (bf16[256,256]{1,0:T(8,128)(2,1)S(1)}, bf16[256,256]{1,0:T(8,128)(2,1)S(1)}, u32[]{:S(2)}, u32[]{:S(2)}) collective-permute-start(bf16[256,256]{1,0:T(8,128)(2,1)S(1)} %collective-permute-done.4), channel_id=1, source_target_pairs={{224,0},{0,32},{32,64},{64,96},{96,128},{128,160},{160,192},{192,2... | collective-permute-start | bytes 393224 | tf_op jit(solution)/shard_map/ppermute | solution.py:12
  128.7 15.2 %collective-permute-start.6 = (bf16[256,256]{1,0:T(8,128)(2,1)S(1)}, bf16[256,256]{1,0:T(8,128)(2,1)S(1)}, u32[]{:S(2)}, u32[]{:S(2)}) collective-permute-start(bf16[256,256]{1,0:T(8,128)(2,1)S(1)} %collective-permute-done.5), channel_id=1, source_target_pairs={{224,0},{0,32},{32,64},{64,96},{96,128},{128,160},{160,192},{192,2... | collective-permute-start | bytes 393224 | tf_op jit(solution)/shard_map/ppermute | solution.py:12
  165.5 130.8 %copy-start.42 = (bf16[256,256]{1,0:T(8,128)(2,1)S(1)}, bf16[256,256]{1,0:T(8,128)(2,1)}, u32[]{:S(2)}) copy-start(bf16[256,256]{1,0:T(8,128)(2,1)} %param.15) | copy-start | bytes 393220
  165.5 388.2 %all-reduce.3.cloned.1.call-start = ((), (), s32[]{:S(2)}) async-start(), calls=%async_computation.3 | async-start | bytes 1048576 | tf_op jit(solution)/shard_map/psum | solution.py:110
  166.6 135.6 %copy-start.22 = (s32[24]{0:T(128)S(1)}, s32[24]{0:T(128)}, u32[]{:S(2)}) copy-start(s32[24]{0:T(128)} %get-tuple-element.35) | copy-start | bytes 292
  166.6 135.6 %copy-start.23 = (s32[24]{0:T(128)S(1)}, s32[24]{0:T(128)}, u32[]{:S(2)}) copy-start(s32[24]{0:T(128)} %get-tuple-element.36) | copy-start | bytes 292
  166.6 135.6 %copy-start.20 = (s32[24]{0:T(128)S(1)}, s32[24]{0:T(128)}, u32[]{:S(2)}) copy-start(s32[24]{0:T(128)} %copy-done.19) | copy-start | bytes 292
  166.6 135.6 %copy-start.21 = (s32[24]{0:T(128)S(1)}, s32[24]{0:T(128)}, u32[]{:S(2)}) copy-start(s32[24]{0:T(128)} %get-tuple-element.34) | copy-start | bytes 292
  296.2 2.9 copy-start.43
  300.1 342.9 %all-gather.2.cloned.1.call-start = ((), (), s32[]{:S(2)}) async-start(), calls=%async_computation.2 | async-start | bytes 4325376 | tf_op jit(solution)/shard_map/all_gather | solution.py:81
  655.6 3.8 copy-start.39
  655.6 17.8 %collective-permute-start.7 = (bf16[256,256]{1,0:T(8,128)(2,1)S(1)}, bf16[256,256]{1,0:T(8,128)(2,1)}, u32[]{:S(2)}, u32[]{:S(2)}) collective-permute-start(bf16[256,256]{1,0:T(8,128)(2,1)S(1)} %bitcast.310), channel_id=1, source_target_pairs={{32,0},{64,32},{96,64},{128,96},{160,128},{192,160},{224,192},{0,2... | collective-permute-start | bytes 393224 | tf_op jit(solution)/shard_map/ppermute | solution.py:12
  674.4 16.1 %collective-permute-start.8 = (bf16[256,256]{1,0:T(8,128)(2,1)S(1)}, bf16[256,256]{1,0:T(8,128)(2,1)}, u32[]{:S(2)}, u32[]{:S(2)}) collective-permute-start(bf16[256,256]{1,0:T(8,128)(2,1)S(1)} %fusion.40), channel_id=1, source_target_pairs={{32,0},{64,32},{96,64},{128,96},{160,128},{192,160},{224,192},{0,2... | collective-permute-start | bytes 393224 | tf_op jit(solution)/shard_map/ppermute | solution.py:12
  691.4 17.2 %collective-permute-start.9 = (bf16[256,256]{1,0:T(8,128)(2,1)S(1)}, bf16[256,256]{1,0:T(8,128)(2,1)}, u32[]{:S(2)}, u32[]{:S(2)}) collective-permute-start(bf16[256,256]{1,0:T(8,128)(2,1)S(1)} %fusion.39), channel_id=1, source_target_pairs={{32,0},{64,32},{96,64},{128,96},{160,128},{192,160},{224,192},{0,2... | collective-permute-start | bytes 393224 | tf_op jit(solution)/shard_map/ppermute | solution.py:12
  704.8 6.5 copy-start.35
  709.6 16.0 %collective-permute-start.10 = (bf16[256,256]{1,0:T(8,128)(2,1)S(1)}, bf16[256,256]{1,0:T(8,128)(2,1)}, u32[]{:S(2)}, u32[]{:S(2)}) collective-permute-start(bf16[256,256]{1,0:T(8,128)(2,1)S(1)} %fusion.38), channel_id=1, source_target_pairs={{32,0},{64,32},{96,64},{128,96},{160,128},{192,160},{224,192},{0,2... | collective-permute-start | bytes 393224 | tf_op jit(solution)/shard_map/ppermute | solution.py:12
  717.8 4.1 copy-start.13
  721.9 5.7 copy-start.33
  726.6 15.3 %collective-permute-start.11 = (bf16[256,256]{1,0:T(8,128)(2,1)S(1)}, bf16[256,256]{1,0:T(8,128)(2,1)}, u32[]{:S(2)}, u32[]{:S(2)}) collective-permute-start(bf16[256,256]{1,0:T(8,128)(2,1)S(1)} %fusion.37), channel_id=1, source_target_pairs={{32,0},{64,32},{96,64},{128,96},{160,128},{192,160},{224,192},{0,2... | collective-permute-start | bytes 393224 | tf_op jit(solution)/shard_map/ppermute | solution.py:12
  734.0 4.1 copy-start.11
  738.1 6.2 copy-start.31
  742.8 15.8 %collective-permute-start.12 = (bf16[256,256]{1,0:T(8,128)(2,1)S(1)}, bf16[256,256]{1,0:T(8,128)(2,1)}, u32[]{:S(2)}, u32[]{:S(2)}) collective-permute-start(bf16[256,256]{1,0:T(8,128)(2,1)S(1)} %fusion.36), channel_id=1, source_target_pairs={{32,0},{64,32},{96,64},{128,96},{160,128},{192,160},{224,192},{0,2... | collective-permute-start | bytes 393224 | tf_op jit(solution)/shard_map/ppermute | solution.py:12
  750.7 4.1 copy-start.9
  754.8 6.2 copy-start.29
  760.2 11.0 %collective-permute-start.13 = (bf16[256,256]{1,0:T(8,128)(2,1)}, bf16[256,256]{1,0:T(8,128)(2,1)}, u32[]{:S(2)}, u32[]{:S(2)}) collective-permute-start(bf16[256,256]{1,0:T(8,128)(2,1)} %fusion.35), channel_id=1, source_target_pairs={{32,0},{64,32},{96,64},{128,96},{160,128},{192,160},{224,192},{0,2... | collective-permute-start | bytes 393224 | tf_op jit(solution)/shard_map/ppermute | solution.py:12
  767.4 5.5 copy-start.1
  (13 other events, 23.2 us)
Sparse Core Ops, SparseCore 0:
  165.6 130.5 reduce-scatter.1
  303.3 250.3 all-reduce.2
  557.5 85.4 all-gather.1
where the time goes:
time: 790 us; the launch traced here: 780 us
  waiting for transfers between devices  467 us (59%)
  other arithmetic  128 us (16%)
  local copies, waits for them, and re-layouts  84.9 us (11%)
  matrix products  64.5 us (8%)
  starting transfers between devices  20.9 us (3%)
  between operations  15 us (2%)
    psum x1, waiting for transfers between devices, per_device(): lax.psum((local_self, local_neigh), ('blk', 'grp'))  250 us
    reduce_scatter x1, waiting for transfers between devices, per_device(): lax.psum_scatter(partial_rows, 'grp', scatter_dimension=0, tiled=True)  130 us
    all_gather x1, waiting for transfers between devices, per_device(): lax.all_gather(grad_slab, 'grp', axis=0, tiled=True)  86.5 us
    scatter-add x8, other arithmetic, slab_kernel(): return running.at[block_places // col_count].add(products)  70.1 us
    dot_general x8, matrix products, class_kernel(): jnp.einsum('jab,jaf->jbf', block_values, picked, preferred_element_type=j...  31.3 us
    gather x8, local copies, waits for them, and re-layouts, class_kernel(): picked = grad_tiles[block_places // col_count]  30.6 us
    scatter-add x8, other arithmetic, class_kernel(): return running.at[block_places % col_count].add(products)  30.2 us
    dot_general x8, matrix products, slab_kernel(): jnp.einsum('jab,jbf->jaf', block_values, picked, preferred_element_type=j...  27.3 us
  transfers between devices with their start and end apart: 17, of which 3 were waited for; matrix products, arithmetic and copies ran while one was open for 29% of the time, Pallas kernels for 0%

commit v1 on v0

v1 whole, which is shorter than its diff:
```python
import math

import jax
import jax.numpy as jnp
from jax import lax
from jax.experimental import pallas as pl
from jax.experimental.pallas import tpu as pltpu
from jax.sharding import PartitionSpec as P

BF16 = jnp.bfloat16
F32 = jnp.float32
GROUP = 4
MIB = 1 << 20
SMEM = pl.BlockSpec(memory_space=pltpu.SMEM)
VMEM = pl.BlockSpec(memory_space=pltpu.VMEM)
ANY = pl.BlockSpec(memory_space=pl.ANY)

RING = 8


def along_grp(x, where):
    def target(i):
        z, y, c = where(i // 4, i // 2 % 2, i % 2)
        return z % RING * 4 + y * 2 + c

    return lax.ppermute(x, "grp", [(i, target(i)) for i in range(4 * RING)])


def other_core(x):
    return along_grp(x, lambda z, y, c: (z, y, 1 - c))


def other_y(x):
    return along_grp(x, lambda z, y, c: (z, 1 - y, c))


def along_z(x, distance):
    return along_grp(x, lambda z, y, c: (z + distance, y, c))


def flip_z(x, bit):
    return along_grp(x, lambda z, y, c: (z ^ bit, y, c))


def along_blk(x, distance):
    n = lax.axis_size("blk")
    return lax.ppermute(x, "blk", [(i, (i + distance) % n) for i in range(n)])


def flip_blk(x, bit):
    n = lax.axis_size("blk")
    return lax.ppermute(x, "blk", [(i, i ^ bit) for i in range(n)])


def chunk_of(me, order, same_y, same_core):
    z, y, c = me // 4, me // 2 % 2, me % 2
    z = lax.rem(z + order + RING, RING)
    y = y if same_y else 1 - y
    c = c if same_core else 1 - c
    return z * 4 + y * 2 + c


def placed(block, col, live):
    zero = jnp.zeros_like(block)
    left = jnp.where(jnp.logical_and(live, col == 0), block, zero)
    right = jnp.where(jnp.logical_and(live, col == 1), block, zero)
    return left, right


def slab_kernel(me_ref, pos_ref, counts_ref, blocks_ref, *refs):
    feats, (send_y, send_k, keep_y, keep_k, acc, held, sems) = refs[:8], refs[8:]
    lists, slots = pos_ref.shape
    copies = [
        pltpu.make_async_copy(blocks_ref.at[k], held.at[k], sems.at[k]) for k in range(lists)
    ]
    for copy in copies:
        copy.start()

    def clear(i, _):
        acc[i] = jnp.zeros(acc.shape[1:], F32)
        return 0

    lax.fori_loop(0, acc.shape[0], clear, 0)
    for k in range(lists):
        copies[k].wait()
        live = counts_ref[k]
        feat = feats[k][...]

        def step(s, _, k=k, live=live, feat=feat):
            rows, places = [], []
            for u in range(GROUP):
                j = s * GROUP + u
                p = pos_ref[k, j]
                left, right = placed(held[k, j], p % 2, j < live)
                rows.append(jnp.concatenate([left, right], axis=1))
                places.append(p // 2)
            products = jnp.dot(jnp.concatenate(rows, axis=0), feat, preferred_element_type=F32)
            tile = rows[0].shape[0]
            for u in range(GROUP):
                acc[places[u]] += products[u * tile : (u + 1) * tile]
            return 0

        lax.fori_loop(0, (live + GROUP - 1) // GROUP, step, 0)
    me = me_ref[0]
    tile = acc.shape[1]
    for out, same_y, same_core in (
        (send_y, False, False),
        (send_k, True, False),
        (keep_y, False, True),
        (keep_k, True, True),
    ):

        def write(i, _, out=out, same_y=same_y, same_core=same_core):
            chunk = chunk_of(me, i, same_y, same_core)
            for half in range(2):
                start = pl.multiple_of((i * 2 + half) * tile, tile)
                out[pl.ds(start, tile), :] = acc[chunk * 2 + half].astype(BF16)
            return 0

        lax.fori_loop(0, RING, write, 0)


def slab_sums(me, block_pos, counts, blocks, feats):
    lists, slots, tile, _ = blocks.shape
    rows, width = feats[0].shape
    quarter = jax.ShapeDtypeStruct((RING * rows, width), BF16)
    return pl.pallas_call(
        slab_kernel,
        out_shape=(quarter,) * 4,
        in_specs=[SMEM, SMEM, SMEM, ANY] + [VMEM] * lists,
        out_specs=(VMEM,) * 4,
        scratch_shapes=[
            pltpu.VMEM((4 * RING * rows // tile, tile, width), F32),
            pltpu.VMEM(blocks.shape, BF16),
            pltpu.SemaphoreType.DMA((lists,)),
        ],
        compiler_params=pltpu.CompilerParams(vmem_limit_bytes=28 * MIB),
        cost_estimate=pl.CostEstimate(
            flops=4 * lists * slots * tile * tile * width,
            bytes_accessed=14 * MIB,
            transcendentals=0,
        ),
        name="slab_sums",
    )(me, block_pos, counts, blocks, *feats)


def mid_kernel(refs_in, refs_out):
    feats, cotangent, degree, w_self, w_neigh, parts = refs_in
    out, grad_slab, grad_self, local_self, local_neigh = refs_out
    deg = degree[...]
    summed = parts[0][...].astype(F32)
    for part in parts[1:]:
        summed = summed + part[...].astype(F32)
    mean = (summed / deg).astype(BF16)
    x, ws, wn = feats[...], w_self[...], w_neigh[...]
    pre = jnp.dot(x, ws, preferred_element_type=F32) + jnp.dot(mean, wn, preferred_element_type=F32)
    sigma = jax.nn.sigmoid(pre)
    out[...] = (pre * sigma).astype(BF16)
    grad = (cotangent[...].astype(F32) * sigma * (1.0 + pre * (1.0 - sigma))).astype(BF16)
    transposed = (((1,), (1,)), ((), ()))
    back = lax.dot_general(grad, wn, transposed, preferred_element_type=F32)
    grad_slab[...] = (back / deg).astype(BF16)
    grad_self[...] = lax.dot_general(grad, ws, transposed, preferred_element_type=F32)
    over_rows = (((0,), (0,)), ((), ()))
    local_self[...] = lax.dot_general(x, grad, over_rows, preferred_element_type=F32).astype(BF16)
    local_neigh[...] = lax.dot_general(mean, grad, over_rows, preferred_element_type=F32).astype(
        BF16
    )


def middle(feats, cotangent, degree, w_self, w_neigh, parts):
    rows, width = feats.shape

    def kernel(*refs):
        mid_kernel((*refs[:5], refs[5 : 5 + len(parts)]), refs[5 + len(parts) :])

    low, wide = jax.ShapeDtypeStruct((rows, width), BF16), jax.ShapeDtypeStruct((rows, width), F32)
    square = jax.ShapeDtypeStruct((width, width), BF16)
    return pl.pallas_call(
        kernel,
        out_shape=(low, low, wide, square, square),
        in_specs=[VMEM] * (5 + len(parts)),
        out_specs=(VMEM,) * 5,
        compiler_params=pltpu.CompilerParams(vmem_limit_bytes=16 * MIB),
        cost_estimate=pl.CostEstimate(
            flops=12 * rows * width * width, bytes_accessed=4 * MIB, transcendentals=rows * width
        ),
        name="middle",
    )(feats, cotangent, degree, w_self, w_neigh, *parts)


def class_kernel(me_ref, pos_ref, counts_ref, blocks_ref, *refs):
    lists, slots = pos_ref.shape
    pieces, (other, far), outs = refs[:RING], refs[RING : RING + 2], refs[RING + 2 : RING + 2 + lists]
    grads, held, sems = refs[RING + 2 + lists :]
    copies = [
        pltpu.make_async_copy(blocks_ref.at[k], held.at[k], sems.at[k]) for k in range(lists)
    ]
    for copy in copies:
        copy.start()
    me = me_ref[0]
    rows = pieces[0].shape[0]
    tile = grads.shape[1]

    def put(chunk, value):
        for half in range(2):
            grads[chunk * 2 + half] = value[half * tile : (half + 1) * tile]

    for i in range(RING):
        put(chunk_of(me, -i, True, True), pieces[i][...])
    for source, first, same_y, same_core in (
        (other, 0, False, True),
        (far, 0, True, False),
        (far, RING, False, False),
    ):

        def place(i, _, source=source, first=first, same_y=same_y, same_core=same_core):
            start = pl.multiple_of((first + i) * rows, rows)
            put(chunk_of(me, -i, same_y, same_core), source[pl.ds(start, rows), :])
            return 0

        lax.fori_loop(0, RING, place, 0)
    for k in range(lists):
        copies[k].wait()
        live = counts_ref[k]

        def step(s, total, k=k, live=live):
            cols, picked = [], []
            for u in range(GROUP):
                j = s * GROUP + u
                p = pos_ref[k, j]
                top, bottom = placed(held[k, j].T, p % 2, j < live)
                cols.append(jnp.concatenate([top, bottom], axis=0))
                picked.append(grads[p // 2])
            return total + jnp.dot(
                jnp.concatenate(cols, axis=1),
                jnp.concatenate(picked, axis=0),
                preferred_element_type=F32,
            )

        outs[k][...] = lax.fori_loop(
            0, (live + GROUP - 1) // GROUP, step, jnp.zeros(outs[k].shape, F32)
        ).astype(outs[k].dtype)


def class_sums(me, block_pos, counts, blocks, pieces, other, far):
    lists, slots, tile, _ = blocks.shape
    rows, width = pieces[0].shape
    return pl.pallas_call(
        class_kernel,
        out_shape=[jax.ShapeDtypeStruct((rows, width), BF16)] * lists,
        in_specs=[SMEM, SMEM, SMEM, ANY] + [VMEM] * (RING + 2),
        out_specs=[VMEM] * lists,
        scratch_shapes=[
            pltpu.VMEM((4 * RING * rows // tile, tile, width), BF16),
            pltpu.VMEM(blocks.shape, BF16),
            pltpu.SemaphoreType.DMA((lists,)),
        ],
        compiler_params=pltpu.CompilerParams(vmem_limit_bytes=28 * MIB),
        cost_estimate=pl.CostEstimate(
            flops=4 * lists * slots * tile * tile * width,
            bytes_accessed=14 * MIB,
            transcendentals=0,
        ),
        name="class_sums",
    )(me, block_pos, counts, blocks, *pieces, other, far)


def added(*terms):
    total = terms[0].astype(F32)
    for term in terms[1:]:
        total = total + term.astype(F32)
    return total.astype(BF16)


def per_device(features, blocks, block_pos, counts, degree, w_self, w_neigh, cotangent):
    cycle_size = lax.axis_size("blk")
    group_size = lax.axis_size("grp")
    rows, width = features.shape
    place = lax.axis_index("grp").astype(jnp.int32)
    me = place.reshape(1)
    block_values, block_places, live_counts = blocks[0, 0], block_pos[0, 0], counts[0, 0]

    feats = [features] + [along_blk(features, k) for k in range(1, cycle_size)]
    send_y, send_k, keep_y, keep_k = slab_sums(me, block_places, live_counts, block_values, feats)
    y_sum = added(keep_y, other_core(send_y))
    k_recv = other_core(send_k)
    y_recv = other_y(y_sum)

    def z_part(i):
        at = slice(i * rows, (i + 1) * rows)
        return added(keep_k[at], k_recv[at], y_recv[at])

    parts = [z_part(0)] + [along_z(z_part(i), i) for i in range(1, RING)]
    scale_deg = degree.astype(F32)[:, None]
    out, grad_slab, grad_self, local_self, local_neigh = middle(
        features, cotangent, scale_deg, w_self, w_neigh, parts
    )

    pieces = [grad_slab] + [along_z(grad_slab, i) for i in range(1, RING)]
    own = jnp.concatenate(pieces, axis=0)
    other = other_y(own)
    far = other_core(jnp.concatenate([own, other], axis=0))
    terms = class_sums(me, block_places, live_counts, block_values, pieces, other, far)
    sums = [terms[0]] + [along_blk(terms[k], -k) for k in range(1, cycle_size)]
    back_sum = grad_self
    for term in sums:
        back_sum = back_sum + term.astype(F32)
    grad_x = back_sum.astype(BF16)

    first = place % 2 == 0
    total = added(
        jnp.where(first, local_self, local_neigh),
        other_core(jnp.where(first, local_neigh, local_self)),
    )
    for bit in (1, 2, 4):
        total = added(total, flip_z(total, bit))
    total = added(total, other_y(total))
    for bit in (1, 2, 4):
        total = added(total, flip_blk(total, bit))
    twin = other_core(total)
    norm_scale = 1.0 / math.sqrt(rows * cycle_size * group_size)
    total_self = jnp.where(first, total, twin).astype(F32) * norm_scale
    total_neigh = jnp.where(first, twin, total).astype(F32) * norm_scale
    return (out, grad_x, total_self, total_neigh)


def solution(mesh):
    in_specs = (
        P(("blk", "grp"), None),
        P("blk", "grp", None, None, None, None),
        P("blk", "grp", None, None),
        P("blk", "grp", None),
        P(("blk", "grp")),
        P(),
        P(),
        P(("blk", "grp"), None),
    )
    out_specs = (P(("blk", "grp"), None), P(("blk", "grp"), None), P(), P())
    return jax.shard_map(
        per_device, mesh=mesh, in_specs=in_specs, out_specs=out_specs, check_vma=False
    )
```

time: 790 us -> 237 us (0.30)
  waiting for transfers between devices: 467 us -> 115 us
  other arithmetic: 128 us -> 2.7 us
  local copies, waits for them, and re-layouts: 84.9 us -> 15.7 us
  matrix products: 64.5 us -> 0 us
  starting transfers between devices: 20.9 us -> 79.6 us
  Pallas kernels: 0 us -> 21 us
  between operations: 15 us -> 0.85 us
    psum x1 -> x0, waiting for transfers between devices: 250 us -> none  [per_device(): lax.psum((local_self, local_neigh), ('blk', 'grp'))]
    reduce_scatter x1 -> x0, waiting for transfers between devices: 130 us -> none  [per_device(): lax.psum_scatter(partial_rows, 'grp', scatter_dimension=0, tiled=True)]
    ppermute x14 -> x42, waiting for transfers between devices: 0.04 us -> 115 us  [the longest x25 90.2 us: along_grp(): return lax.ppermute(x, 'grp', [(i, target(i)) for i in range(4 * RING)])]
    scatter-add x16 -> x0, other arithmetic: 100 us -> none  [the longest x8 70.1 us: slab_kernel(): return running.at[block_places // col_count].add(products)]
    all_gather x1 -> x0, waiting for transfers between devices: 86.5 us -> none  [per_device(): lax.all_gather(grad_slab, 'grp', axis=0, tiled=True)]
    dot_general x22 -> x0, matrix products: 64.5 us -> none  [the longest x8 31.3 us: class_kernel(): jnp.einsum('jab,jaf->jbf', block_values, picked, preferred_element_type=j...]
    ppermute x14 -> x42, starting transfers between devices: 20.8 us -> 79.6 us  [the longest x25 45.9 us: along_grp(): return lax.ppermute(x, 'grp', [(i, target(i)) for i in range(4 * RING)])]
    gather x16 -> x0, local copies, waits for them, and re-layouts: 38.1 us -> none  [the longest x8 30.6 us: class_kernel(): picked = grad_tiles[block_places // col_count]]
  transfers between devices with their start and end apart: 17 -> 42, of which waited for: 3 -> 27; matrix products, arithmetic and copies ran while one was open for 29% -> 3% of each run, Pallas kernels for 0% -> 4%
where the time goes in v1:
time: 237 us; the launch traced here: 234 us
  waiting for transfers between devices  115 us (49%)
  starting transfers between devices  79.6 us (34%)
  Pallas kernels  21 us (9%)
  local copies, waits for them, and re-layouts  15.7 us (7%)
  other arithmetic  2.7 us (1%)
    ppermute x25, waiting for transfers between devices, along_grp(): return lax.ppermute(x, 'grp', [(i, target(i)) for i in range(4 * RING)])  90.2 us
    ppermute x25, starting transfers between devices, along_grp(): return lax.ppermute(x, 'grp', [(i, target(i)) for i in range(4 * RING)])  45.9 us
    ppermute x14, starting transfers between devices, along_blk(): return lax.ppermute(x, 'blk', [(i, (i + distance) % n) for i in range(n)])  28.6 us
    ppermute x3, waiting for transfers between devices, flip_blk(): return lax.ppermute(x, 'blk', [(i, i ^ bit) for i in range(n)])  15.2 us
    unnamed x34, local copies, waits for them, and re-layouts  14.5 us
    pallas_call x1, Pallas kernels, class_sums(): pl.pallas_call(class_kernel, out_shape=[jax.ShapeDtypeStruct((rows, width...  10 us
    pallas_call x1, Pallas kernels, slab_sums(): pl.pallas_call(slab_kernel, out_shape=(quarter,) * 4, in_specs=[SMEM, SME...  9.98 us
    ppermute x14, waiting for transfers between devices, along_blk(): return lax.ppermute(x, 'blk', [(i, (i + distance) % n) for i in range(n)])  9.16 us
  transfers between devices with their start and end apart: 42, of which 27 were waited for; matrix products, arithmetic and copies ran while one was open for 3% of the time, Pallas kernels for 4%

profile of v1, /device:TPU:2, one launch (start us, length us, event | category | flops | bytes accessed | tf_op | source)
XLA Modules:
  0.0 234.5 jit_solution(7228500412390602192)
XLA Ops:
  0.6 1.7 collective-permute-start
  2.3 1.5 collective-permute-start.1
  3.8 2.7 %collective-permute-start.2 = (bf16[256,256]{1,0:T(8,128)(2,1)}, bf16[256,256]{1,0:T(8,128)(2,1)S(1)}, u32[]{:S(2)}, u32[]{:S(2)}) collective-permute-start(bf16[256,256]{1,0:T(8,128)(2,1)} %refs_0_.3), channel_id=1, source_target_pairs={{0,96},{32,128},{64,160},{96,192},{128,224},{160,0},{192,32},{224,... | collective-permute-start | bytes 393224 | tf_op jit(solution)/shard_map/ppermute | solution.py:47
  7.2 2.4 %collective-permute-start.4 = (bf16[256,256]{1,0:T(8,128)(2,1)}, bf16[256,256]{1,0:T(8,128)(2,1)S(1)}, u32[]{:S(2)}, u32[]{:S(2)}) collective-permute-start(bf16[256,256]{1,0:T(8,128)(2,1)} %refs_0_.3), channel_id=1, source_target_pairs={{0,160},{32,192},{64,224},{96,0},{128,32},{160,64},{192,96},{224,1... | collective-permute-start | bytes 393224 | tf_op jit(solution)/shard_map/ppermute | solution.py:47
  9.6 1.9 collective-permute-start.5
  12.9 1.7 collective-permute-done.3.refs_4_
  14.6 2.2 collective-permute-done.4.refs_5_
  16.8 1.6 collective-permute-done.5.refs_6_
  19.5 2.8 %copy-done.5 = bf16[1,1,8,24,128,128]{5,4,3,2,1,0:T(8,128)(2,1)S(1)} copy-done((bf16[1,1,8,24,128,128]{5,4,3,2,1,0:T(8,128)(2,1)S(1)}, bf16[1,1,8,24,128,128]{5,4,3,2,1,0:T(8,128)(2,1)}, u32[]{:S(2)}) %copy-start.5) | copy-done | bytes 6291480
  23.6 10.0 %slab_sums.1 = (bf16[2048,256]{1,0:T(8,128)(2,1)S(1)}, bf16[2048,256]{1,0:T(8,128)(2,1)S(1)}, bf16[2048,256]{1,0:T(8,128)(2,1)S(1)}, bf16[2048,256]{1,0:T(8,128)(2,1)S(1)}) custom-call(s32[1]{0:T(128)} %bitcast.1.me_ref, s32[8,24]{1,0:T(8,128)S(1)} %bitcast.7, s32[8]{0:T(128)S(1)} %bitcast.9, bf16[8,24,128,128]{3,2,1,0:T(8,128)(2,1)S(1)} %bitcast.5, ...), custom_call_target="tpu_custom_call" | custom-call | flops 3221225472 | bytes 14680064 | tf_op jit(solution)/shard_map/slab_sums/pallas_call | solution.py:127
  34.2 2.1 collective-permute-done.8
  36.6 2.5 %collective-permute-start.9 = (bf16[2048,256]{1,0:T(8,128)(2,1)S(1)}, bf16[2048,256]{1,0:T(8,128)(2,1)S(1)}, u32[]{:S(2)}, u32[]{:S(2)}) collective-permute-start(bf16[2048,256]{1,0:T(8,128)(2,1)S(1)} %add_convert_fusion), channel_id=1, source_target_pairs={{0,2},{1,3},{2,0},{3,1},{4,6},{5,7},{6,4},{7,5},{8,10},{9,11},{10,... | collective-permute-start | bytes 3145736 | tf_op jit(solution)/shard_map/ppermute | solution.py:26
  39.1 24.3 %collective-permute-done.9 = bf16[2048,256]{1,0:T(8,128)(2,1)S(1)} collective-permute-done((bf16[2048,256]{1,0:T(8,128)(2,1)S(1)}, bf16[2048,256]{1,0:T(8,128)(2,1)S(1)}, u32[]{:S(2)}, u32[]{:S(2)}) %collective-permute-start.9) | collective-permute-done | bytes 1048608 | tf_op jit(solution)/shard_map/ppermute | solution.py:26
  65.1 3.9 %collective-permute-start.11 = (bf16[256,256]{1,0:T(8,128)(2,1)S(1)}, bf16[256,256]{1,0:T(8,128)(2,1)S(1)}, u32[]{:S(2)}, u32[]{:S(2)}) collective-permute-start(bf16[256,256]{1,0:T(8,128)(2,1)S(1)} %get-tuple-element.43), channel_id=1, source_target_pairs={{0,8},{1,9},{2,10},{3,11},{4,12},{5,13},{6,14},{7,15},{8,16},{9,17... | collective-permute-start | bytes 393224 | tf_op jit(solution)/shard_map/ppermute | solution.py:26
  69.0 4.0 %collective-permute-start.12 = (bf16[256,256]{1,0:T(8,128)(2,1)S(1)}, bf16[256,256]{1,0:T(8,128)(2,1)S(1)}, u32[]{:S(2)}, u32[]{:S(2)}) collective-permute-start(bf16[256,256]{1,0:T(8,128)(2,1)S(1)} %get-tuple-element.42), channel_id=1, source_target_pairs={{0,12},{1,13},{2,14},{3,15},{4,16},{5,17},{6,18},{7,19},{8,20},{9,... | collective-permute-start | bytes 393224 | tf_op jit(solution)/shard_map/ppermute | solution.py:26
  73.0 1.7 collective-permute-start.13
  74.7 2.8 %collective-permute-start.14 = (bf16[256,256]{1,0:T(8,128)(2,1)S(1)}, bf16[256,256]{1,0:T(8,128)(2,1)S(1)}, u32[]{:S(2)}, u32[]{:S(2)}) collective-permute-start(bf16[256,256]{1,0:T(8,128)(2,1)S(1)} %get-tuple-element.40), channel_id=1, source_target_pairs={{0,20},{1,21},{2,22},{3,23},{4,24},{5,25},{6,26},{7,27},{8,28},{9,... | collective-permute-start | bytes 393224 | tf_op jit(solution)/shard_map/ppermute | solution.py:26
  77.5 3.3 %collective-permute-start.15 = (bf16[256,256]{1,0:T(8,128)(2,1)S(1)}, bf16[256,256]{1,0:T(8,128)(2,1)S(1)}, u32[]{:S(2)}, u32[]{:S(2)}) collective-permute-start(bf16[256,256]{1,0:T(8,128)(2,1)S(1)} %get-tuple-element.39), channel_id=1, source_target_pairs={{0,24},{1,25},{2,26},{3,27},{4,28},{5,29},{6,30},{7,31},{8,0},{9,1... | collective-permute-start | bytes 393224 | tf_op jit(solution)/shard_map/ppermute | solution.py:26
  81.6 2.7 %collective-permute-start.16 = (bf16[256,256]{1,0:T(8,128)(2,1)S(1)}, bf16[256,256]{1,0:T(8,128)(2,1)S(1)}, u32[]{:S(2)}, u32[]{:S(2)}) collective-permute-start(bf16[256,256]{1,0:T(8,128)(2,1)S(1)} %get-tuple-element.38), channel_id=1, source_target_pairs={{0,28},{1,29},{2,30},{3,31},{4,0},{5,1},{6,2},{7,3},{8,4},{9,5},{1... | collective-permute-start | bytes 393224 | tf_op jit(solution)/shard_map/ppermute | solution.py:26
  84.5 3.2 %collective-permute-done.12.refs_8_ = bf16[256,256]{1,0:T(8,128)(2,1)S(1)} collective-permute-done((bf16[256,256]{1,0:T(8,128)(2,1)S(1)}, bf16[256,256]{1,0:T(8,128)(2,1)S(1)}, u32[]{:S(2)}, u32[]{:S(2)}) %collective-permute-start.12) | collective-permute-done | bytes 131104 | tf_op jit(solution)/shard_map/ppermute | solution.py:26
  87.7 4.1 %collective-permute-done.13.refs_9_ = bf16[256,256]{1,0:T(8,128)(2,1)S(1)} collective-permute-done((bf16[256,256]{1,0:T(8,128)(2,1)S(1)}, bf16[256,256]{1,0:T(8,128)(2,1)S(1)}, u32[]{:S(2)}, u32[]{:S(2)}) %collective-permute-start.13) | collective-permute-done | bytes 131104 | tf_op jit(solution)/shard_map/ppermute | solution.py:26
  91.8 2.0 collective-permute-done.14.refs_10_
  93.9 2.7 %collective-permute-done.15.refs_11_ = bf16[256,256]{1,0:T(8,128)(2,1)S(1)} collective-permute-done((bf16[256,256]{1,0:T(8,128)(2,1)S(1)}, bf16[256,256]{1,0:T(8,128)(2,1)S(1)}, u32[]{:S(2)}, u32[]{:S(2)}) %collective-permute-start.15) | collective-permute-done | bytes 131104 | tf_op jit(solution)/shard_map/ppermute | solution.py:26
  96.6 1.6 collective-permute-done.16.refs_12_
  99.2 2.0 collective-permute-start.17
  103.4 4.8 %collective-permute-start.20 = (bf16[256,256]{1,0:T(8,128)(2,1)S(1)}, bf16[256,256]{1,0:T(8,128)(2,1)S(1)}, u32[]{:S(2)}, u32[]{:S(2)}) collective-permute-start(bf16[256,256]{1,0:T(8,128)(2,1)S(1)} %get-tuple-element.27.refs_0_), channel_id=1, source_target_pairs={{0,16},{1,17},{2,18},{3,19},{4,20},{5,21},{6,22},{7,23},{8,24},{9,... | collective-permute-start | bytes 393224 | tf_op jit(solution)/shard_map/ppermute | solution.py:26
  108.2 2.5 %collective-permute-start.21 = (bf16[256,256]{1,0:T(8,128)(2,1)S(1)}, bf16[256,256]{1,0:T(8,128)(2,1)S(1)}, u32[]{:S(2)}, u32[]{:S(2)}) collective-permute-start(bf16[256,256]{1,0:T(8,128)(2,1)S(1)} %get-tuple-element.27.refs_0_), channel_id=1, source_target_pairs={{0,20},{1,21},{2,22},{3,23},{4,24},{5,25},{6,26},{7,27},{8,28},{9,... | collective-permute-start | bytes 393224 | tf_op jit(solution)/shard_map/ppermute | solution.py:26
  113.4 5.4 %collective-permute-done.18.refs_2_ = bf16[256,256]{1,0:T(8,128)(2,1)S(1)} collective-permute-done((bf16[256,256]{1,0:T(8,128)(2,1)S(1)}, bf16[256,256]{1,0:T(8,128)(2,1)S(1)}, u32[]{:S(2)}, u32[]{:S(2)}) %collective-permute-start.18) | collective-permute-done | bytes 131104 | tf_op jit(solution)/shard_map/ppermute | solution.py:26
  120.1 2.5 %collective-permute-done.20.refs_4_ = bf16[256,256]{1,0:T(8,128)(2,1)S(1)} collective-permute-done((bf16[256,256]{1,0:T(8,128)(2,1)S(1)}, bf16[256,256]{1,0:T(8,128)(2,1)S(1)}, u32[]{:S(2)}, u32[]{:S(2)}) %collective-permute-start.20) | collective-permute-done | bytes 131104 | tf_op jit(solution)/shard_map/ppermute | solution.py:26
  124.5 4.3 %collective-permute-done.22.refs_6_ = bf16[256,256]{1,0:T(8,128)(2,1)S(1)} collective-permute-done((bf16[256,256]{1,0:T(8,128)(2,1)S(1)}, bf16[256,256]{1,0:T(8,128)(2,1)S(1)}, u32[]{:S(2)}, u32[]{:S(2)}) %collective-permute-start.22) | collective-permute-done | bytes 131104 | tf_op jit(solution)/shard_map/ppermute | solution.py:26
  129.5 1.6 collective-permute-done.23.refs_7_
  133.1 2.6 %collective-permute-start.24 = (bf16[2048,256]{1,0:T(8,128)(2,1)}, bf16[2048,256]{1,0:T(8,128)(2,1)S(1)}, u32[]{:S(2)}, u32[]{:S(2)}) collective-permute-start(bf16[2048,256]{1,0:T(8,128)(2,1)} %get-tuple-element.49), channel_id=1, source_target_pairs={{0,2},{1,3},{2,0},{3,1},{4,6},{5,7},{6,4},{7,5},{8,10},{9,11},{10,... | collective-permute-start | bytes 3145736 | tf_op jit(solution)/shard_map/ppermute | solution.py:26
  138.5 4.3 %collective-permute-done.34 = bf16[256,256]{1,0:T(8,128)(2,1)S(1)} collective-permute-done((bf16[256,256]{1,0:T(8,128)(2,1)S(1)}, bf16[256,256]{1,0:T(8,128)(2,1)S(1)}, u32[]{:S(2)}, u32[]{:S(2)}) %collective-permute-start.34) | collective-permute-done | bytes 131104 | tf_op jit(solution)/shard_map/ppermute | solution.py:26
  142.8 2.3 %collective-permute-start.35 = (bf16[256,256]{1,0:T(8,128)(2,1)S(1)}, bf16[256,256]{1,0:T(8,128)(2,1)S(1)}, u32[]{:S(2)}, u32[]{:S(2)}) collective-permute-start(bf16[256,256]{1,0:T(8,128)(2,1)S(1)} %add_convert_fusion.7), channel_id=1, source_target_pairs={{0,8},{1,9},{2,10},{3,11},{4,12},{5,13},{6,14},{7,15},{8,0},{9,1},... | collective-permute-start | bytes 393224 | tf_op jit(solution)/shard_map/ppermute | solution.py:26
  145.2 14.1 %collective-permute-done.24.refs_8_ = bf16[2048,256]{1,0:T(8,128)(2,1)S(1)} collective-permute-done((bf16[2048,256]{1,0:T(8,128)(2,1)}, bf16[2048,256]{1,0:T(8,128)(2,1)S(1)}, u32[]{:S(2)}, u32[]{:S(2)}) %collective-permute-start.24) | collective-permute-done | bytes 1048608 | tf_op jit(solution)/shard_map/ppermute | solution.py:26
  160.3 3.0 %collective-permute-start.36 = (bf16[256,256]{1,0:T(8,128)(2,1)S(1)}, bf16[256,256]{1,0:T(8,128)(2,1)S(1)}, u32[]{:S(2)}, u32[]{:S(2)}) collective-permute-start(bf16[256,256]{1,0:T(8,128)(2,1)S(1)} %add_convert_fusion.6), channel_id=1, source_target_pairs={{0,16},{1,17},{2,18},{3,19},{4,20},{5,21},{6,22},{7,23},{8,24},{9,... | collective-permute-start | bytes 393224 | tf_op jit(solution)/shard_map/ppermute | solution.py:26
  163.3 9.6 %collective-permute-done.36 = bf16[256,256]{1,0:T(8,128)(2,1)S(1)} collective-permute-done((bf16[256,256]{1,0:T(8,128)(2,1)S(1)}, bf16[256,256]{1,0:T(8,128)(2,1)S(1)}, u32[]{:S(2)}, u32[]{:S(2)}) %collective-permute-start.36) | collective-permute-done | bytes 131104 | tf_op jit(solution)/shard_map/ppermute | solution.py:26
  173.9 5.7 %collective-permute-done.37 = bf16[256,256]{1,0:T(8,128)(2,1)S(1)} collective-permute-done((bf16[256,256]{1,0:T(8,128)(2,1)S(1)}, bf16[256,256]{1,0:T(8,128)(2,1)S(1)}, u32[]{:S(2)}, u32[]{:S(2)}) %collective-permute-start.37) | collective-permute-done | bytes 131104 | tf_op jit(solution)/shard_map/ppermute | solution.py:26
  179.6 4.9 %collective-permute-start.38 = (bf16[256,256]{1,0:T(8,128)(2,1)S(1)}, bf16[256,256]{1,0:T(8,128)(2,1)S(1)}, u32[]{:S(2)}, u32[]{:S(2)}) collective-permute-start(bf16[256,256]{1,0:T(8,128)(2,1)S(1)} %add_convert_fusion.4), channel_id=1, source_target_pairs={{0,32},{32,0},{64,96},{96,64},{128,160},{160,128},{192,224},{224,1... | collective-permute-start | bytes 393224 | tf_op jit(solution)/shard_map/ppermute | solution.py:52
  184.5 2.9 %collective-permute-done.38 = bf16[256,256]{1,0:T(8,128)(2,1)S(1)} collective-permute-done((bf16[256,256]{1,0:T(8,128)(2,1)S(1)}, bf16[256,256]{1,0:T(8,128)(2,1)S(1)}, u32[]{:S(2)}, u32[]{:S(2)}) %collective-permute-start.38) | collective-permute-done | bytes 131104 | tf_op jit(solution)/shard_map/ppermute | solution.py:52
  187.6 5.8 %collective-permute-done.39 = bf16[256,256]{1,0:T(8,128)(2,1)S(1)} collective-permute-done((bf16[256,256]{1,0:T(8,128)(2,1)S(1)}, bf16[256,256]{1,0:T(8,128)(2,1)S(1)}, u32[]{:S(2)}, u32[]{:S(2)}) %collective-permute-start.39) | collective-permute-done | bytes 131104 | tf_op jit(solution)/shard_map/ppermute | solution.py:52
  193.5 6.5 %collective-permute-done.40 = bf16[256,256]{1,0:T(8,128)(2,1)S(1)} collective-permute-done((bf16[256,256]{1,0:T(8,128)(2,1)S(1)}, bf16[256,256]{1,0:T(8,128)(2,1)S(1)}, u32[]{:S(2)}, u32[]{:S(2)}) %collective-permute-start.40) | collective-permute-done | bytes 131104 | tf_op jit(solution)/shard_map/ppermute | solution.py:52
  200.2 2.8 %copy-done.6 = bf16[1,1,8,24,128,128]{5,4,3,2,1,0:T(8,128)(2,1)S(1)} copy-done((bf16[1,1,8,24,128,128]{5,4,3,2,1,0:T(8,128)(2,1)S(1)}, bf16[1,1,8,24,128,128]{5,4,3,2,1,0:T(8,128)(2,1)}, u32[]{:S(2)}) %copy-start.6) | copy-done | bytes 6291480
  203.0 10.0 %class_sums.1 = (bf16[256,256]{1,0:T(8,128)(2,1)S(1)}, bf16[256,256]{1,0:T(8,128)(2,1)S(1)}, bf16[256,256]{1,0:T(8,128)(2,1)S(1)}, bf16[256,256]{1,0:T(8,128)(2,...) custom-call(s32[1]{0:T(128)} %bitcast.1.me_ref, ...), custom_call_target="tpu_custom_call" | custom-call | flops 3221225472 | bytes 14680064 | tf_op jit(solution)/shard_map/class_sums/pallas_call | solution.py:249
  213.8 3.4 %collective-permute-start.30 = (bf16[256,256]{1,0:T(8,128)(2,1)S(1)}, bf16[256,256]{1,0:T(8,128)(2,1)S(1)}, u32[]{:S(2)}, u32[]{:S(2)}) collective-permute-start(bf16[256,256]{1,0:T(8,128)(2,1)S(1)} %get-tuple-element.33), channel_id=1, source_target_pairs={{0,96},{32,128},{64,160},{96,192},{128,224},{160,0},{192,32},{224,... | collective-permute-start | bytes 393224 | tf_op jit(solution)/shard_map/ppermute | solution.py:47
  218.1 3.5 %collective-permute-start.28 = (bf16[256,256]{1,0:T(8,128)(2,1)S(1)}, bf16[256,256]{1,0:T(8,128)(2,1)S(1)}, u32[]{:S(2)}, u32[]{:S(2)}) collective-permute-start(bf16[256,256]{1,0:T(8,128)(2,1)S(1)} %get-tuple-element.31), channel_id=1, source_target_pairs={{0,160},{32,192},{64,224},{96,0},{128,32},{160,64},{192,96},{224,1... | collective-permute-start | bytes 393224 | tf_op jit(solution)/shard_map/ppermute | solution.py:47
  221.6 8.4 %collective-permute-start.26 = (bf16[256,256]{1,0:T(8,128)(2,1)S(1)}, bf16[256,256]{1,0:T(8,128)(2,1)S(1)}, u32[]{:S(2)}, u32[]{:S(2)}) collective-permute-start(bf16[256,256]{1,0:T(8,128)(2,1)S(1)} %get-tuple-element.29), channel_id=1, source_target_pairs={{0,224},{32,0},{64,32},{96,64},{128,96},{160,128},{192,160},{224,1... | collective-permute-start | bytes 393224 | tf_op jit(solution)/shard_map/ppermute | solution.py:47
  230.9 2.8 %collective-permute-done.26 = bf16[256,256]{1,0:T(8,128)(2,1)S(1)} collective-permute-done((bf16[256,256]{1,0:T(8,128)(2,1)S(1)}, bf16[256,256]{1,0:T(8,128)(2,1)S(1)}, u32[]{:S(2)}, u32[]{:S(2)}) %collective-permute-start.26) | collective-permute-done | bytes 131104 | tf_op jit(solution)/shard_map/ppermute | solution.py:47
  (90 shorter events, 28.6 us)
Async XLA Ops:
  0.6 8.9 %collective-permute-start = (bf16[256,256]{1,0:T(8,128)(2,1)}, bf16[256,256]{1,0:T(8,128)(2,1)S(1)}, u32[]{:S(2)}, u32[]{:S(2)}) collective-permute-start(bf16[256,256]{1,0:T(8,128)(2,1)} %refs_0_.3), channel_id=1, source_target_pairs={{0,32},{32,64},{64,96},{96,128},{128,160},{160,192},{192,224},{224... | collective-permute-start | bytes 393224 | tf_op jit(solution)/shard_map/ppermute | solution.py:47
  2.3 9.2 %collective-permute-start.1 = (bf16[256,256]{1,0:T(8,128)(2,1)}, bf16[256,256]{1,0:T(8,128)(2,1)S(1)}, u32[]{:S(2)}, u32[]{:S(2)}) collective-permute-start(bf16[256,256]{1,0:T(8,128)(2,1)} %refs_0_.3), channel_id=1, source_target_pairs={{0,64},{32,96},{64,128},{96,160},{128,192},{160,224},{192,0},{224,... | collective-permute-start | bytes 393224 | tf_op jit(solution)/shard_map/ppermute | solution.py:47
  3.8 9.1 %collective-permute-start.2 = (bf16[256,256]{1,0:T(8,128)(2,1)}, bf16[256,256]{1,0:T(8,128)(2,1)S(1)}, u32[]{:S(2)}, u32[]{:S(2)}) collective-permute-start(bf16[256,256]{1,0:T(8,128)(2,1)} %refs_0_.3), channel_id=1, source_target_pairs={{0,96},{32,128},{64,160},{96,192},{128,224},{160,0},{192,32},{224,... | collective-permute-start | bytes 393224 | tf_op jit(solution)/shard_map/ppermute | solution.py:47
  6.5 8.1 %collective-permute-start.3 = (bf16[256,256]{1,0:T(8,128)(2,1)}, bf16[256,256]{1,0:T(8,128)(2,1)S(1)}, u32[]{:S(2)}, u32[]{:S(2)}) collective-permute-start(bf16[256,256]{1,0:T(8,128)(2,1)} %refs_0_.3), channel_id=1, source_target_pairs={{0,128},{32,160},{64,192},{96,224},{128,0},{160,32},{192,64},{224,... | collective-permute-start | bytes 393224 | tf_op jit(solution)/shard_map/ppermute | solution.py:47
  7.2 9.6 %collective-permute-start.4 = (bf16[256,256]{1,0:T(8,128)(2,1)}, bf16[256,256]{1,0:T(8,128)(2,1)S(1)}, u32[]{:S(2)}, u32[]{:S(2)}) collective-permute-start(bf16[256,256]{1,0:T(8,128)(2,1)} %refs_0_.3), channel_id=1, source_target_pairs={{0,160},{32,192},{64,224},{96,0},{128,32},{160,64},{192,96},{224,1... | collective-permute-start | bytes 393224 | tf_op jit(solution)/shard_map/ppermute | solution.py:47
  9.6 8.8 %collective-permute-start.5 = (bf16[256,256]{1,0:T(8,128)(2,1)}, bf16[256,256]{1,0:T(8,128)(2,1)S(1)}, u32[]{:S(2)}, u32[]{:S(2)}) collective-permute-start(bf16[256,256]{1,0:T(8,128)(2,1)} %refs_0_.3), channel_id=1, source_target_pairs={{0,192},{32,224},{64,0},{96,32},{128,64},{160,96},{192,128},{224,1... | collective-permute-start | bytes 393224 | tf_op jit(solution)/shard_map/ppermute | solution.py:47
  11.5 7.1 %collective-permute-start.6 = (bf16[256,256]{1,0:T(8,128)(2,1)}, bf16[256,256]{1,0:T(8,128)(2,1)S(1)}, u32[]{:S(2)}, u32[]{:S(2)}) collective-permute-start(bf16[256,256]{1,0:T(8,128)(2,1)} %refs_0_.3), channel_id=1, source_target_pairs={{0,224},{32,0},{64,32},{96,64},{128,96},{160,128},{192,160},{224,1... | collective-permute-start | bytes 393224 | tf_op jit(solution)/shard_map/ppermute | solution.py:47
  33.6 2.7 %collective-permute-start.8 = (bf16[2048,256]{1,0:T(8,128)(2,1)S(1)}, bf16[2048,256]{1,0:T(8,128)(2,1)S(1)}, u32[]{:S(2)}, u32[]{:S(2)}) collective-permute-start(bf16[2048,256]{1,0:T(8,128)(2,1)S(1)} %get-tuple-element.24), channel_id=1, source_target_pairs={{0,1},{1,0},{2,3},{3,2},{4,5},{5,4},{6,7},{7,6},{8,9},{9,8},{10,11... | collective-permute-start | bytes 3145736 | tf_op jit(solution)/shard_map/ppermute | solution.py:26
  33.7 5.5 %collective-permute-start.7 = (bf16[2048,256]{1,0:T(8,128)(2,1)S(1)}, bf16[2048,256]{1,0:T(8,128)(2,1)S(1)}, u32[]{:S(2)}, u32[]{:S(2)}) collective-permute-start(bf16[2048,256]{1,0:T(8,128)(2,1)S(1)} %get-tuple-element.22), channel_id=1, source_target_pairs={{0,1},{1,0},{2,3},{3,2},{4,5},{5,4},{6,7},{7,6},{8,9},{9,8},{10,11... | collective-permute-start | bytes 3145736 | tf_op jit(solution)/shard_map/ppermute | solution.py:26
  36.6 26.8 %collective-permute-start.9 = (bf16[2048,256]{1,0:T(8,128)(2,1)S(1)}, bf16[2048,256]{1,0:T(8,128)(2,1)S(1)}, u32[]{:S(2)}, u32[]{:S(2)}) collective-permute-start(bf16[2048,256]{1,0:T(8,128)(2,1)S(1)} %add_convert_fusion), channel_id=1, source_target_pairs={{0,2},{1,3},{2,0},{3,1},{4,6},{5,7},{6,4},{7,5},{8,10},{9,11},{10,... | collective-permute-start | bytes 3145736 | tf_op jit(solution)/shard_map/ppermute | solution.py:26
  63.4 34.7 %copy-start.1 = (bf16[256,256]{1,0:T(8,128)(2,1)S(1)}, bf16[256,256]{1,0:T(8,128)(2,1)}, u32[]{:S(2)}) copy-start(bf16[256,256]{1,0:T(8,128)(2,1)} %refs_0_.3) | copy-start | bytes 393220
  63.4 34.7 %copy-start.2 = (bf16[256,256]{1,0:T(8,128)(2,1)S(1)}, bf16[256,256]{1,0:T(8,128)(2,1)}, u32[]{:S(2)}) copy-start(bf16[256,256]{1,0:T(8,128)(2,1)} %refs_1_.1) | copy-start | bytes 393220
  63.4 34.7 %copy-start.3 = (bf16[256,256]{1,0:T(8,128)(2,1)S(1)}, bf16[256,256]{1,0:T(8,128)(2,1)}, u32[]{:S(2)}) copy-start(bf16[256,256]{1,0:T(8,128)(2,1)} %refs_3_.1) | copy-start | bytes 393220
  63.4 34.7 %copy-start.4 = (bf16[256,256]{1,0:T(8,128)(2,1)S(1)}, bf16[256,256]{1,0:T(8,128)(2,1)}, u32[]{:S(2)}) copy-start(bf16[256,256]{1,0:T(8,128)(2,1)} %refs_4_.1) | copy-start | bytes 393220
  63.5 14.0 %collective-permute-start.10 = (bf16[256,256]{1,0:T(8,128)(2,1)S(1)}, bf16[256,256]{1,0:T(8,128)(2,1)S(1)}, u32[]{:S(2)}, u32[]{:S(2)}) collective-permute-start(bf16[256,256]{1,0:T(8,128)(2,1)S(1)} %get-tuple-element.44), channel_id=1, source_target_pairs={{0,4},{1,5},{2,6},{3,7},{4,8},{5,9},{6,10},{7,11},{8,12},{9,13},{1... | collective-permute-start | bytes 393224 | tf_op jit(solution)/shard_map/ppermute | solution.py:26
  65.1 16.6 %collective-permute-start.11 = (bf16[256,256]{1,0:T(8,128)(2,1)S(1)}, bf16[256,256]{1,0:T(8,128)(2,1)S(1)}, u32[]{:S(2)}, u32[]{:S(2)}) collective-permute-start(bf16[256,256]{1,0:T(8,128)(2,1)S(1)} %get-tuple-element.43), channel_id=1, source_target_pairs={{0,8},{1,9},{2,10},{3,11},{4,12},{5,13},{6,14},{7,15},{8,16},{9,17... | collective-permute-start | bytes 393224 | tf_op jit(solution)/shard_map/ppermute | solution.py:26
  69.0 18.7 %collective-permute-start.12 = (bf16[256,256]{1,0:T(8,128)(2,1)S(1)}, bf16[256,256]{1,0:T(8,128)(2,1)S(1)}, u32[]{:S(2)}, u32[]{:S(2)}) collective-permute-start(bf16[256,256]{1,0:T(8,128)(2,1)S(1)} %get-tuple-element.42), channel_id=1, source_target_pairs={{0,12},{1,13},{2,14},{3,15},{4,16},{5,17},{6,18},{7,19},{8,20},{9,... | collective-permute-start | bytes 393224 | tf_op jit(solution)/shard_map/ppermute | solution.py:26
  73.0 18.8 %collective-permute-start.13 = (bf16[256,256]{1,0:T(8,128)(2,1)S(1)}, bf16[256,256]{1,0:T(8,128)(2,1)S(1)}, u32[]{:S(2)}, u32[]{:S(2)}) collective-permute-start(bf16[256,256]{1,0:T(8,128)(2,1)S(1)} %get-tuple-element.41), channel_id=1, source_target_pairs={{0,16},{1,17},{2,18},{3,19},{4,20},{5,21},{6,22},{7,23},{8,24},{9,... | collective-permute-start | bytes 393224 | tf_op jit(solution)/shard_map/ppermute | solution.py:26
  74.7 19.1 %collective-permute-start.14 = (bf16[256,256]{1,0:T(8,128)(2,1)S(1)}, bf16[256,256]{1,0:T(8,128)(2,1)S(1)}, u32[]{:S(2)}, u32[]{:S(2)}) collective-permute-start(bf16[256,256]{1,0:T(8,128)(2,1)S(1)} %get-tuple-element.40), channel_id=1, source_target_pairs={{0,20},{1,21},{2,22},{3,23},{4,24},{5,25},{6,26},{7,27},{8,28},{9,... | collective-permute-start | bytes 393224 | tf_op jit(solution)/shard_map/ppermute | solution.py:26
  77.5 19.1 %collective-permute-start.15 = (bf16[256,256]{1,0:T(8,128)(2,1)S(1)}, bf16[256,256]{1,0:T(8,128)(2,1)S(1)}, u32[]{:S(2)}, u32[]{:S(2)}) collective-permute-start(bf16[256,256]{1,0:T(8,128)(2,1)S(1)} %get-tuple-element.39), channel_id=1, source_target_pairs={{0,24},{1,25},{2,26},{3,27},{4,28},{5,29},{6,30},{7,31},{8,0},{9,1... | collective-permute-start | bytes 393224 | tf_op jit(solution)/shard_map/ppermute | solution.py:26
  81.6 16.5 %collective-permute-start.16 = (bf16[256,256]{1,0:T(8,128)(2,1)S(1)}, bf16[256,256]{1,0:T(8,128)(2,1)S(1)}, u32[]{:S(2)}, u32[]{:S(2)}) collective-permute-start(bf16[256,256]{1,0:T(8,128)(2,1)S(1)} %get-tuple-element.38), channel_id=1, source_target_pairs={{0,28},{1,29},{2,30},{3,31},{4,0},{5,1},{6,2},{7,3},{8,4},{9,5},{1... | collective-permute-start | bytes 393224 | tf_op jit(solution)/shard_map/ppermute | solution.py:26
  99.2 12.2 %collective-permute-start.17 = (bf16[256,256]{1,0:T(8,128)(2,1)S(1)}, bf16[256,256]{1,0:T(8,128)(2,1)S(1)}, u32[]{:S(2)}, u32[]{:S(2)}) collective-permute-start(bf16[256,256]{1,0:T(8,128)(2,1)S(1)} %get-tuple-element.27.refs_0_), channel_id=1, source_target_pairs={{0,4},{1,5},{2,6},{3,7},{4,8},{5,9},{6,10},{7,11},{8,12},{9,13},{1... | collective-permute-start | bytes 393224 | tf_op jit(solution)/shard_map/ppermute | solution.py:26
  101.2 17.6 %collective-permute-start.18 = (bf16[256,256]{1,0:T(8,128)(2,1)S(1)}, bf16[256,256]{1,0:T(8,128)(2,1)S(1)}, u32[]{:S(2)}, u32[]{:S(2)}) collective-permute-start(bf16[256,256]{1,0:T(8,128)(2,1)S(1)} %get-tuple-element.27.refs_0_), channel_id=1, source_target_pairs={{0,8},{1,9},{2,10},{3,11},{4,12},{5,13},{6,14},{7,15},{8,16},{9,17... | collective-permute-start | bytes 393224 | tf_op jit(solution)/shard_map/ppermute | solution.py:26
  102.4 17.1 %collective-permute-start.19 = (bf16[256,256]{1,0:T(8,128)(2,1)S(1)}, bf16[256,256]{1,0:T(8,128)(2,1)S(1)}, u32[]{:S(2)}, u32[]{:S(2)}) collective-permute-start(bf16[256,256]{1,0:T(8,128)(2,1)S(1)} %get-tuple-element.27.refs_0_), channel_id=1, source_target_pairs={{0,12},{1,13},{2,14},{3,15},{4,16},{5,17},{6,18},{7,19},{8,20},{9,... | collective-permute-start | bytes 393224 | tf_op jit(solution)/shard_map/ppermute | solution.py:26
  103.4 19.2 %collective-permute-start.20 = (bf16[256,256]{1,0:T(8,128)(2,1)S(1)}, bf16[256,256]{1,0:T(8,128)(2,1)S(1)}, u32[]{:S(2)}, u32[]{:S(2)}) collective-permute-start(bf16[256,256]{1,0:T(8,128)(2,1)S(1)} %get-tuple-element.27.refs_0_), channel_id=1, source_target_pairs={{0,16},{1,17},{2,18},{3,19},{4,20},{5,21},{6,22},{7,23},{8,24},{9,... | collective-permute-start | bytes 393224 | tf_op jit(solution)/shard_map/ppermute | solution.py:26
  108.2 15.6 %collective-permute-start.21 = (bf16[256,256]{1,0:T(8,128)(2,1)S(1)}, bf16[256,256]{1,0:T(8,128)(2,1)S(1)}, u32[]{:S(2)}, u32[]{:S(2)}) collective-permute-start(bf16[256,256]{1,0:T(8,128)(2,1)S(1)} %get-tuple-element.27.refs_0_), channel_id=1, source_target_pairs={{0,20},{1,21},{2,22},{3,23},{4,24},{5,25},{6,26},{7,27},{8,28},{9,... | collective-permute-start | bytes 393224 | tf_op jit(solution)/shard_map/ppermute | solution.py:26
  111.4 17.3 %collective-permute-start.22 = (bf16[256,256]{1,0:T(8,128)(2,1)S(1)}, bf16[256,256]{1,0:T(8,128)(2,1)S(1)}, u32[]{:S(2)}, u32[]{:S(2)}) collective-permute-start(bf16[256,256]{1,0:T(8,128)(2,1)S(1)} %get-tuple-element.27.refs_0_), channel_id=1, source_target_pairs={{0,24},{1,25},{2,26},{3,27},{4,28},{5,29},{6,30},{7,31},{8,0},{9,1... | collective-permute-start | bytes 393224 | tf_op jit(solution)/shard_map/ppermute | solution.py:26
  118.8 12.3 %collective-permute-start.23 = (bf16[256,256]{1,0:T(8,128)(2,1)S(1)}, bf16[256,256]{1,0:T(8,128)(2,1)S(1)}, u32[]{:S(2)}, u32[]{:S(2)}) collective-permute-start(bf16[256,256]{1,0:T(8,128)(2,1)S(1)} %get-tuple-element.27.refs_0_), channel_id=1, source_target_pairs={{0,28},{1,29},{2,30},{3,31},{4,0},{5,1},{6,2},{7,3},{8,4},{9,5},{1... | collective-permute-start | bytes 393224 | tf_op jit(solution)/shard_map/ppermute | solution.py:26
  133.1 26.2 %collective-permute-start.24 = (bf16[2048,256]{1,0:T(8,128)(2,1)}, bf16[2048,256]{1,0:T(8,128)(2,1)S(1)}, u32[]{:S(2)}, u32[]{:S(2)}) collective-permute-start(bf16[2048,256]{1,0:T(8,128)(2,1)} %get-tuple-element.49), channel_id=1, source_target_pairs={{0,2},{1,3},{2,0},{3,1},{4,6},{5,7},{6,4},{7,5},{8,10},{9,11},{10,... | collective-permute-start | bytes 3145736 | tf_op jit(solution)/shard_map/ppermute | solution.py:26
  135.7 1.4 collective-permute-start.33
  137.1 5.6 %collective-permute-start.34 = (bf16[256,256]{1,0:T(8,128)(2,1)S(1)}, bf16[256,256]{1,0:T(8,128)(2,1)S(1)}, u32[]{:S(2)}, u32[]{:S(2)}) collective-permute-start(bf16[256,256]{1,0:T(8,128)(2,1)S(1)} %add_convert_fusion.8), channel_id=1, source_target_pairs={{0,4},{1,5},{2,6},{3,7},{4,0},{5,1},{6,2},{7,3},{8,12},{9,13},{10,... | collective-permute-start | bytes 393224 | tf_op jit(solution)/shard_map/ppermute | solution.py:26
  142.8 17.5 %collective-permute-start.35 = (bf16[256,256]{1,0:T(8,128)(2,1)S(1)}, bf16[256,256]{1,0:T(8,128)(2,1)S(1)}, u32[]{:S(2)}, u32[]{:S(2)}) collective-permute-start(bf16[256,256]{1,0:T(8,128)(2,1)S(1)} %add_convert_fusion.7), channel_id=1, source_target_pairs={{0,8},{1,9},{2,10},{3,11},{4,12},{5,13},{6,14},{7,15},{8,0},{9,1},... | collective-permute-start | bytes 393224 | tf_op jit(solution)/shard_map/ppermute | solution.py:26
  159.2 40.9 %copy-start.8 = (s32[1,1,8,24]{3,2,1,0:T(8,128)S(1)}, s32[1,1,8,24]{3,2,1,0:T(8,128)}, u32[]{:S(2)}) copy-start(s32[1,1,8,24]{3,2,1,0:T(8,128)} %param.10) | copy-start | bytes 2308
  159.2 40.9 %copy-start.10 = (s32[1,1,8]{2,1,0:T(1,128)S(1)}, s32[1,1,8]{2,1,0:T(1,128)}, u32[]{:S(2)}) copy-start(s32[1,1,8]{2,1,0:T(1,128)} %param.11) | copy-start | bytes 100
  160.3 39.8 %collective-permute-start.25 = (bf16[4096,256]{1,0:T(8,128)(2,1)}, bf16[4096,256]{1,0:T(8,128)(2,1)S(1)}, u32[]{:S(2)}, u32[]{:S(2)}) collective-permute-start(bf16[4096,256]{1,0:T(8,128)(2,1)} %constant_dynamic-update-slice_fusion.8), channel_id=1, source_target_pairs={{0,1},{1,0},{2,3},{3,2},{4,5},{5,4},{6,7},{7,6},{8,9},{9,8},{10,11... | collective-permute-start | bytes 6291464 | tf_op jit(solution)/shard_map/ppermute | solution.py:26
  160.3 12.6 %collective-permute-start.36 = (bf16[256,256]{1,0:T(8,128)(2,1)S(1)}, bf16[256,256]{1,0:T(8,128)(2,1)S(1)}, u32[]{:S(2)}, u32[]{:S(2)}) collective-permute-start(bf16[256,256]{1,0:T(8,128)(2,1)S(1)} %add_convert_fusion.6), channel_id=1, source_target_pairs={{0,16},{1,17},{2,18},{3,19},{4,20},{5,21},{6,22},{7,23},{8,24},{9,... | collective-permute-start | bytes 393224 | tf_op jit(solution)/shard_map/ppermute | solution.py:26
  173.0 6.6 %collective-permute-start.37 = (bf16[256,256]{1,0:T(8,128)(2,1)S(1)}, bf16[256,256]{1,0:T(8,128)(2,1)S(1)}, u32[]{:S(2)}, u32[]{:S(2)}) collective-permute-start(bf16[256,256]{1,0:T(8,128)(2,1)S(1)} %add_convert_fusion.5), channel_id=1, source_target_pairs={{0,2},{1,3},{2,0},{3,1},{4,6},{5,7},{6,4},{7,5},{8,10},{9,11},{10,... | collective-permute-start | bytes 393224 | tf_op jit(solution)/shard_map/ppermute | solution.py:26
  179.6 7.9 %collective-permute-start.38 = (bf16[256,256]{1,0:T(8,128)(2,1)S(1)}, bf16[256,256]{1,0:T(8,128)(2,1)S(1)}, u32[]{:S(2)}, u32[]{:S(2)}) collective-permute-start(bf16[256,256]{1,0:T(8,128)(2,1)S(1)} %add_convert_fusion.4), channel_id=1, source_target_pairs={{0,32},{32,0},{64,96},{96,64},{128,160},{160,128},{192,224},{224,1... | collective-permute-start | bytes 393224 | tf_op jit(solution)/shard_map/ppermute | solution.py:52
  187.5 5.9 %collective-permute-start.39 = (bf16[256,256]{1,0:T(8,128)(2,1)S(1)}, bf16[256,256]{1,0:T(8,128)(2,1)S(1)}, u32[]{:S(2)}, u32[]{:S(2)}) collective-permute-start(bf16[256,256]{1,0:T(8,128)(2,1)S(1)} %add_convert_fusion.3), channel_id=1, source_target_pairs={{0,64},{32,96},{64,0},{96,32},{128,192},{160,224},{192,128},{224,1... | collective-permute-start | bytes 393224 | tf_op jit(solution)/shard_map/ppermute | solution.py:52
  193.4 6.6 %collective-permute-start.40 = (bf16[256,256]{1,0:T(8,128)(2,1)S(1)}, bf16[256,256]{1,0:T(8,128)(2,1)S(1)}, u32[]{:S(2)}, u32[]{:S(2)}) collective-permute-start(bf16[256,256]{1,0:T(8,128)(2,1)S(1)} %add_convert_fusion.2), channel_id=1, source_target_pairs={{0,128},{32,160},{64,192},{96,224},{128,0},{160,32},{192,64},{224,... | collective-permute-start | bytes 393224 | tf_op jit(solution)/shard_map/ppermute | solution.py:52
  200.0 18.0 %collective-permute-start.41 = (bf16[256,256]{1,0:T(8,128)(2,1)S(1)}, bf16[256,256]{1,0:T(8,128)(2,1)S(1)}, u32[]{:S(2)}, u32[]{:S(2)}) collective-permute-start(bf16[256,256]{1,0:T(8,128)(2,1)S(1)} %add_convert_fusion.1), channel_id=1, source_target_pairs={{0,1},{1,0},{2,3},{3,2},{4,5},{5,4},{6,7},{7,6},{8,9},{9,8},{10,11... | collective-permute-start | bytes 393224 | tf_op jit(solution)/shard_map/ppermute | solution.py:26
  213.0 8.6 %collective-permute-start.32 = (bf16[256,256]{1,0:T(8,128)(2,1)S(1)}, bf16[256,256]{1,0:T(8,128)(2,1)S(1)}, u32[]{:S(2)}, u32[]{:S(2)}) collective-permute-start(bf16[256,256]{1,0:T(8,128)(2,1)S(1)} %get-tuple-element.35), channel_id=1, source_target_pairs={{0,32},{32,64},{64,96},{96,128},{128,160},{160,192},{192,224},{224... | collective-permute-start | bytes 393224 | tf_op jit(solution)/shard_map/ppermute | solution.py:47
  213.7 7.9 %collective-permute-start.31 = (bf16[256,256]{1,0:T(8,128)(2,1)S(1)}, bf16[256,256]{1,0:T(8,128)(2,1)S(1)}, u32[]{:S(2)}, u32[]{:S(2)}) collective-permute-start(bf16[256,256]{1,0:T(8,128)(2,1)S(1)} %get-tuple-element.34), channel_id=1, source_target_pairs={{0,64},{32,96},{64,128},{96,160},{128,192},{160,224},{192,0},{224,... | collective-permute-start | bytes 393224 | tf_op jit(solution)/shard_map/ppermute | solution.py:47
  213.8 17.0 %collective-permute-start.30 = (bf16[256,256]{1,0:T(8,128)(2,1)S(1)}, bf16[256,256]{1,0:T(8,128)(2,1)S(1)}, u32[]{:S(2)}, u32[]{:S(2)}) collective-permute-start(bf16[256,256]{1,0:T(8,128)(2,1)S(1)} %get-tuple-element.33), channel_id=1, source_target_pairs={{0,96},{32,128},{64,160},{96,192},{128,224},{160,0},{192,32},{224,... | collective-permute-start | bytes 393224 | tf_op jit(solution)/shard_map/ppermute | solution.py:47
  217.3 13.6 %collective-permute-start.29 = (bf16[256,256]{1,0:T(8,128)(2,1)S(1)}, bf16[256,256]{1,0:T(8,128)(2,1)S(1)}, u32[]{:S(2)}, u32[]{:S(2)}) collective-permute-start(bf16[256,256]{1,0:T(8,128)(2,1)S(1)} %get-tuple-element.32), channel_id=1, source_target_pairs={{0,128},{32,160},{64,192},{96,224},{128,0},{160,32},{192,64},{224,... | collective-permute-start | bytes 393224 | tf_op jit(solution)/shard_map/ppermute | solution.py:47
  218.1 12.8 %collective-permute-start.28 = (bf16[256,256]{1,0:T(8,128)(2,1)S(1)}, bf16[256,256]{1,0:T(8,128)(2,1)S(1)}, u32[]{:S(2)}, u32[]{:S(2)}) collective-permute-start(bf16[256,256]{1,0:T(8,128)(2,1)S(1)} %get-tuple-element.31), channel_id=1, source_target_pairs={{0,160},{32,192},{64,224},{96,0},{128,32},{160,64},{192,96},{224,1... | collective-permute-start | bytes 393224 | tf_op jit(solution)/shard_map/ppermute | solution.py:47
  221.5 9.3 %collective-permute-start.27 = (bf16[256,256]{1,0:T(8,128)(2,1)S(1)}, bf16[256,256]{1,0:T(8,128)(2,1)S(1)}, u32[]{:S(2)}, u32[]{:S(2)}) collective-permute-start(bf16[256,256]{1,0:T(8,128)(2,1)S(1)} %get-tuple-element.30), channel_id=1, source_target_pairs={{0,192},{32,224},{64,0},{96,32},{128,64},{160,96},{192,128},{224,1... | collective-permute-start | bytes 393224 | tf_op jit(solution)/shard_map/ppermute | solution.py:47
  221.6 12.1 %collective-permute-start.26 = (bf16[256,256]{1,0:T(8,128)(2,1)S(1)}, bf16[256,256]{1,0:T(8,128)(2,1)S(1)}, u32[]{:S(2)}, u32[]{:S(2)}) collective-permute-start(bf16[256,256]{1,0:T(8,128)(2,1)S(1)} %get-tuple-element.29), channel_id=1, source_target_pairs={{0,224},{32,0},{64,32},{96,64},{128,96},{160,128},{192,160},{224,1... | collective-permute-start | bytes 393224 | tf_op jit(solution)/shard_map/ppermute | solution.py:47
  (7 other events, 30.1 us)
